TPU v7x, 256 devices: a whole 4x4x8 slice. The times are simulated.
256 devices in a mesh: fsdp: 32 (over y, z), tp: 8 (over x, core).
Axes of the slice: x: 4, y: 4, z: 8, core: 2. Of those that a mesh axis runs over, the one named last changes fastest.
Arguments:
- momentum: float32 [8192, 26624], P('fsdp', 'tp'), may hold values from -122 to 122, as said below
- gradient: bfloat16 [8192, 26624], P('fsdp', 'tp'), may hold values from -6 to 6
- basis: float32 [256, 26624], P('fsdp', 'tp'), may hold values from -0.0390625 to 0.0390625
Outputs:
- new_momentum: float32 [8192, 26624], P('fsdp', 'tp')
- new_basis: float32 [256, 26624], P('fsdp', 'tp')
- step: bfloat16 [8192, 26624], P('fsdp', 'tp')
Inputs may be any that keep to these rules, and one draw needn't show every extreme that they name: `momentum`: momentum entries are finite real values.
All inputs are finite; a program needn't handle non-finite values.
Results may differ from a plain program's by a relative error of at most 0.004.
Values sent between devices are 32-bit elements; how exact they have to be, the bound alone decides.
A program may use at most 64 MiB of HBM per device.

v0:
```python
import jax
import jax.numpy as jnp
from jax import lax
from jax.sharding import PartitionSpec as P

ROWS = 8192
COLS = 26624
RANK = 256


momentum_decay = 0.95
norm_eps = 1e-06


def mat(left, right):
    return jnp.dot(left, right, precision=lax.Precision.HIGHEST, preferred_element_type=jnp.float32)


def orthogonal(projected, gram_matrix):
    factor = jnp.linalg.cholesky(gram_matrix)
    return lax.linalg.triangular_solve(
        factor, projected, left_side=False, lower=True, transpose_a=True
    )


def on_device(momentum, gradient, basis):
    buffer = momentum + gradient.astype(jnp.float32)
    share_rank = basis.shape[0]
    partial_proj = mat(buffer, lax.all_gather(basis, "fsdp", axis=0, tiled=True).T)
    projected = lax.psum(partial_proj, "tp")
    gram_matrix = lax.psum(mat(projected.T, projected), "fsdp")
    ortho_basis = orthogonal(projected, gram_matrix)
    coeffs = lax.psum(mat(ortho_basis.T, buffer), "fsdp")
    squares = lax.psum(jnp.sum(coeffs * coeffs, axis=1), "tp")
    inverse_norm = lax.rsqrt(squares + norm_eps)
    first_row = lax.axis_index("fsdp") * share_rank
    own_coeffs = lax.dynamic_slice_in_dim(coeffs, first_row, share_rank, 0)
    own_inverse = lax.dynamic_slice_in_dim(inverse_norm, first_row, share_rank, 0)
    new_basis = own_coeffs * own_inverse[:, None]
    new_momentum = buffer - (1.0 - momentum_decay) * mat(ortho_basis, coeffs)
    scale = (ROWS * COLS / RANK) ** 0.5
    step = (scale * mat(ortho_basis * inverse_norm[None, :], coeffs)).astype(jnp.bfloat16)
    return (new_momentum, new_basis, step)


def solution(mesh):
    placed = (P("fsdp", "tp"), P("fsdp", "tp"), P("fsdp", "tp"))
    return jax.shard_map(
        on_device,
        mesh=mesh,
        in_specs=placed,
        out_specs=(P("fsdp", "tp"), P("fsdp", "tp"), P("fsdp", "tp")),
        check_vma=False,
    )
```

profile of v0, /device:TPU:1, one launch (start us, length us, event | category | flops | bytes accessed | tf_op | source)
XLA Modules:
  0.0 585.5 jit_solution(10810558540008258911)
XLA Ops:
  7.2 0.7 all-gather.2.cloned.1.call-update
  7.9 83.5 %all-gather.2.cloned.1.call-done = f32[256,3328]{1,0:T(8,128)} async-done(((f32[8,3328]{1,0:T(8,128)}), f32[256,3328]{1,0:T(8,128)}) %all-gather.2.cloned.1.call-update) | async-done | bytes 3407888 | tf_op jit(solution)/shard_map/all_gather | solution.py:29
  91.5 7.3 %fusion.3 = f32[256,256]{1,0:T(8,128)} fusion(f32[256,3328]{1,0:T(8,128)} %all-gather.2.cloned.1.call-done, f32[256,3328]{1,0:T(8,128)} %param.3, bf16[256,3328]{1,0:T(8,128)(2,1)} %param.4), kind=kOutput, calls=%fused_computation.9 | convolution fusion | flops 2618949632 | bytes 8781824 | tf_op jit(solution)/shard_map/dot_general | solution.py:16
  98.8 62.9 %all-reduce.5.cloned.1.call-done = f32[256,256]{1,0:T(8,128)} async-done(((f32[256,256]{1,0:T(8,128)}), f32[256,256]{1,0:T(8,128)}) %all-reduce.5.cloned.1.call-update) | async-done | bytes 262160 | tf_op jit(solution)/shard_map/psum | solution.py:30
  161.7 2.3 fusion.18
  164.3 142.9 %all-reduce.7.cloned.1.call-done = f32[256,256]{0,1:T(8,128)} async-done(((f32[256,256]{0,1:T(8,128)}), f32[256,256]{0,1:T(8,128)}) %all-reduce.7.cloned.1.call-update) | async-done | bytes 262160 | tf_op jit(solution)/shard_map/psum | solution.py:31
  307.2 1.8 copy.7
  309.0 1.1 fusion.4
  310.1 0.7 copy-done.6
  310.8 11.7 %cholesky.50 = f32[128,128]{1,0:T(8,128)S(1)} custom-call(f32[128,128]{1,0:T(8,128)S(1)} %cholesky.118), custom_call_target="Cholesky" | custom-call | tf_op jit(solution)/shard_map/jit(cholesky)/cholesky | solution.py:20
  322.5 10.4 %custom-call.14 = f32[1,128,128]{1,2,0:T(8,128)} custom-call(f32[1,128,128]{2,1,0:T(8,128)S(1)} %get-tuple-element.24), custom_call_target="InvertDiagBlocksLowerTriangular" | custom-call | tf_op jit(solution)/shard_map/jit(cholesky)/cholesky | solution.py:20
  333.0 0.7 cholesky.113
  333.7 1.7 constant_dynamic-update-slice_fusion
  335.4 1.1 convolution_subtract_fusion.1
  336.5 11.7 %cholesky.105 = f32[128,128]{1,0:T(8,128)S(1)} custom-call(f32[128,128]{1,0:T(8,128)S(1)} %convolution_subtract_fusion.1), custom_call_target="Cholesky" | custom-call | tf_op jit(solution)/shard_map/jit(cholesky)/cholesky | solution.py:20
  348.2 0.6 select_reduce_fusion
  350.8 1.7 select_select_fusion
  352.6 7.0 %while.1 = (s32[]{:T(128)}, f32[256,256]{1,0:T(8,128)}, s32[2,2]{1,0:T(2,128)S(1)}, f32[2,128,128]{2,1,0:T(8,128)}, s32[]{:T(128)}) while((s32[]{:T(128)}, f32[256,256]{1,0:T(8,128)}, s32[2,2]{1,0:T(2,128)S(1)}, f32[2,128,128]{2,1,0:T(8,128)}, s32[]{:T(128)}) %tuple.27), condition=%wide.while_cond, body=%wide.while_body.sunk | while | flops 2 | bytes 132205 | solution.py:21
  353.2 2.9 bitcast_dynamic-update-slice_fusion.2
  356.7 2.8 bitcast_dynamic-update-slice_fusion.2
  359.5 21.1 %custom-call.15 = f32[2,128,128]{1,2,0:T(8,128)} custom-call(f32[2,128,128]{2,1,0:T(8,128)} %get-tuple-element.10), custom_call_target="InvertDiagBlocksLowerTriangular" | custom-call | tf_op jit(solution)/shard_map/triangular_solve | solution.py:21
  380.6 1.2 fusion.6
  381.8 1.3 convolution_subtract_fusion
  383.2 1.2 fusion.9
  384.4 0.6 copy-done.4
  385.0 6.2 %fusion.2 = f32[256,3328]{1,0:T(8,128)} fusion(f32[256,3328]{1,0:T(8,128)S(1)} %copy-done.1, bf16[256,3328]{1,0:T(8,128)(2,1)} %param.4, f32[256,128]{0,1:T(8,128)S(1)} %fusion.9, f32[256,128]{0,1:T(8,128)S(1)} %fusion.6), kind=kOutput, calls=%fused_computation.8 | convolution fusion | flops 2619015168 | bytes 8781824 | tf_op jit(solution)/shard_map/dot_general | solution.py:16
  391.2 157.4 %all-reduce.9.cloned.1.call-done = f32[256,3328]{1,0:T(8,128)} async-done(((f32[256,3328]{1,0:T(8,128)}), f32[256,3328]{1,0:T(8,128)}) %all-reduce.9.cloned.1.call-update) | async-done | bytes 3407888 | tf_op jit(solution)/shard_map/psum | solution.py:33
  548.7 2.4 multiply_reduce_fusion
  551.1 16.4 %psum.31 = f32[256]{0:T(256)S(1)} all-reduce(f32[256]{0:T(256)S(1)} %multiply_reduce_fusion), channel_id=1, replica_groups=mesh['fsdp'=32,'tp'=8] {'tp'}, use_global_device_ids=true, to_apply=%region_8.9 | all-reduce | flops 256 | bytes 2048 | tf_op jit(solution)/shard_map/psum | solution.py:34
  567.6 5.5 fusion.1
  573.1 5.2 fusion
  578.3 0.7 dynamic-slice_multiply_fusion
  (31 shorter events, 2.4 us)
Async XLA Ops:
  7.2 84.3 %all-gather.2.cloned.1.call-start = ((), (), s32[]{:S(2)}) async-start(), calls=%async_computation | async-start | bytes 3514368 | tf_op jit(solution)/shard_map/all_gather | solution.py:29
  7.9 153.8 %all-reduce.5.cloned.1.call-start = ((), (), s32[]{:S(2)}) async-start(), calls=%async_computation.1 | async-start | bytes 524288 | tf_op jit(solution)/shard_map/psum | solution.py:30
  98.7 286.3 %copy-start.1 = (f32[256,3328]{1,0:T(8,128)S(1)}, f32[256,3328]{1,0:T(8,128)}, u32[]{:S(2)}) copy-start(f32[256,3328]{1,0:T(8,128)} %param.3) | copy-start | bytes 10223620
  98.8 208.4 %all-reduce.7.cloned.1.call-start = ((), (), s32[]{:S(2)}) async-start(), calls=%async_computation.2 | async-start | bytes 524288 | tf_op jit(solution)/shard_map/psum | solution.py:31
  164.1 384.6 %all-reduce.9.cloned.1.call-start = ((), (), s32[]{:S(2)}) async-start(), calls=%async_computation.3 | async-start | bytes 6815744 | tf_op jit(solution)/shard_map/psum | solution.py:33
  310.1 0.7 copy-start.6
  384.3 0.7 copy-start.4
  548.7 18.9 %copy-start = (f32[256,3328]{1,0:T(8,128)S(1)}, f32[256,3328]{1,0:T(8,128)}, u32[]{:S(2)}) copy-start(f32[256,3328]{1,0:T(8,128)} %all-reduce.9.cloned.1.call-done) | copy-start | bytes 10223620
  567.5 5.6 copy-start.2
  567.5 5.6 copy-start.3
  567.5 5.6 copy-start.5
Sparse Core Ops, SparseCore 0:
  10.6 80.8 all-gather.1
  98.9 62.8 all-reduce.4
  166.2 140.9 all-reduce.6
  391.4 157.2 all-reduce.8
where the time goes:
time: 586 us
  waiting for transfers between devices  447 us (76%)
  other arithmetic  62.2 us (11%)
  matrix products  33 us (6%)
  blocking collectives  16.4 us (3%)
  between operations  15.2 us (3%)
  local copies, waits for them, and re-layouts  11 us (2%)
    psum x1, waiting for transfers between devices, on_device(): coeffs = lax.psum(mat(ortho_basis.T, buffer), 'fsdp')  157 us
    psum x1, waiting for transfers between devices, on_device(): gram_matrix = lax.psum(mat(projected.T, projected), 'fsdp')  143 us
    all_gather x1, waiting for transfers between devices, on_device(): lax.all_gather(basis, 'fsdp', axis=0, tiled=True)  83.5 us
    psum x1, waiting for transfers between devices, on_device(): projected = lax.psum(partial_proj, 'tp')  62.9 us
    another operation x6, other arithmetic, orthogonal(): factor = jnp.linalg.cholesky(gram_matrix)  35.2 us
    dot_general x5, matrix products, mat(): jnp.dot(left, right, precision=lax.Precision.HIGHEST, preferred_element_t...  26.5 us
    another operation x3, other arithmetic, orthogonal(): lax.linalg.triangular_solve(factor, projected, left_side=False, lower=Tru...  22.8 us
    psum x1, blocking collectives, on_device(): squares = lax.psum(jnp.sum(coeffs * coeffs, axis=1), 'tp')  16.4 us
  transfers between devices with their start and end apart: 4, of which 4 were waited for; matrix products, arithmetic and copies ran while one was open for 0% of the time, Pallas kernels for 0%

commit v1 on v0

v1 whole, which is shorter than its diff:
```python
import functools

import jax
import jax.numpy as jnp
from jax import lax
from jax.experimental import pallas as pl
from jax.experimental.pallas import tpu as pltpu
from jax.sharding import PartitionSpec as P

ROWS = 8192
COLS = 26624
RANK = 256

momentum_decay = 0.95
norm_eps = 1e-06

Y, Z, T = 4, 8, 8
F = Y * Z
M = ROWS // F
N = COLS // T
R = RANK // F
BLOCK = 256
NB = 16

CUT = 1536
A = (0, CUT)
A_HALF = ((0, CUT // 2), (CUT // 2, CUT // 2))
B = (CUT, N - CUT)
B_HALF = ((CUT, (N - CUT) // 2), (CUT + (N - CUT) // 2, (N - CUT) // 2))

MESH = pl.DeviceIdType.MESH
f32, bf16 = jnp.float32, jnp.bfloat16


def split(value):
    high = value.astype(bf16)
    return high, (value - high.astype(f32)).astype(bf16)


def dot(left, right, dims=((1,), (0,))):
    return lax.dot_general(left, right, (dims, ((), ())), preferred_element_type=f32)


def dot3(left, right, dims=((1,), (0,))):
    (lh, ll), (rh, rl) = left, right
    return dot(lh, rh, dims) + (dot(lh, rl, dims) + dot(ll, rh, dims))


def exact(left, right, dims=((1,), (0,))):
    return lax.dot_general(
        left, right, (dims, ((), ())), precision=lax.Precision.HIGHEST, preferred_element_type=f32
    )


class Wires:
    def __init__(self, send, recv):
        self.send, self.recv, self.count, self.sent = send, recv, 0, []

    def start(self, src, dst, to):
        copy = pltpu.make_async_remote_copy(
            src_ref=src,
            dst_ref=dst,
            send_sem=self.send.at[self.count],
            recv_sem=self.recv.at[self.count],
            device_id=to,
            device_id_type=MESH,
        )
        self.count += 1
        copy.start()
        self.sent.append(copy)
        return copy

    def drain(self, copies=None):
        for copy in list(self.sent if copies is None else copies):
            copy.wait_send()
            self.sent = [other for other in self.sent if other is not copy]


class Place:
    def __init__(self):
        self.f = lax.axis_index("fsdp")
        self.t = lax.axis_index("tp")
        self.y, self.z = self.f // Z, self.f % Z

    def slot(self, dy, dz):
        return (self.y + dy + Y) % Y * Z + (self.z + dz + Z) % Z

    def along_y(self, d):
        return {"fsdp": self.slot(d, 0)}

    def along_z(self, d):
        return {"fsdp": self.slot(0, d)}

    def along_t(self, d):
        return {"tp": (self.t + d) % T}


def cols(ref, slot, part):
    return ref.at[slot, :, pl.ds(part[0], part[1])]


def gather_steps(place, wires, buf):
    a1, b1, a2, b2 = {}, {}, {}, {}
    a_order = (0, -1, 1, 2)
    b_order = (0, -1, 1, -2, 2, -3, 3, 4)
    at = place.slot

    def send(book, key, slot, part, to):
        book[key] = wires.start(cols(buf, slot, part), cols(buf, slot, part), to)

    def a2_step(i):
        h, k = i // 4 + 1, i % 4
        for side, d in enumerate((1, -1)):
            if h > 1:
                a2[h - 1, k, d].wait_recv()
            part = A_HALF[side] if h == 4 else A
            send(a2, (h, k, d), at(a_order[k], -d * (h - 1)), part, place.along_z(d))

    def b2_step(i):
        h, k = i // 8 + 1, i % 8
        for side, d in enumerate((1, -1)):
            if h == 2:
                b2[1, k, d].wait_recv()
            part = B_HALF[side] if h == 2 else B
            send(b2, (h, k, d), at(-d * (h - 1), b_order[k]), part, place.along_y(d))

    def a1_step(i):
        if i == 0:
            for d in (1, -1):
                send(a1, (1, d), at(0, 0), A, place.along_y(d))
        elif i in (1, 2):
            side, d = i - 1, (1, -1)[i - 1]
            a1[1, d].wait_recv()
            send(a1, (2, d), at(-d, 0), A_HALF[side], place.along_y(d))
        elif i == 3:
            for d in (1, -1):
                a1[2, d].wait_recv()

    def b1_step(i):
        if i == 0:
            for d in (1, -1):
                send(b1, (1, d), at(0, 0), B, place.along_z(d))
        elif i in range(1, 7):
            h, side = (i + 1) // 2, (i + 1) % 2
            d = (1, -1)[side]
            b1[h, d].wait_recv()
            part = B_HALF[side] if h == 3 else B
            send(b1, (h + 1, d), at(0, -d * h), part, place.along_z(d))
        elif i == 7:
            for d in (1, -1):
                b1[4, d].wait_recv()

    def step(i):
        b1_step(i)
        a1_step(i)
        b2_step(i)
        a2_step(i)

    def last():
        for k in range(4):
            for d in (1, -1):
                a2[4, k, d].wait_recv()
        for k in range(8):
            for d in (1, -1):
                b2[2, k, d].wait_recv()

    return [functools.partial(step, i) for i in range(16)] + [last]


def scatter_steps(place, wires, part_sums, result, land_a, land_b):
    a1, b1, a2, b2 = {}, {}, {}, {}
    a_order = (2, 1, -1, 0)
    b_order = (4, 3, -3, 2, -2, 1, -1, 0)
    at = place.slot
    used = {"a": 0, "b": 0}

    def send(book, key, slot, part, to, kind):
        land = land_a if kind == "a" else land_b
        index, offset = used[kind], part[0] - (A if kind == "a" else B)[0]
        used[kind] += 1
        target = land.at[index, :, pl.ds(offset, part[1])]
        book[key] = (wires.start(cols(part_sums, slot, part), target, to), target, part)

    def add(book, key, slot):
        copy, target, part = book[key]
        copy.wait_recv()
        own = cols(part_sums, slot, part)
        own[...] += target[...]

    def a1_step(i):
        h, k = i // 4 + 1, i % 4
        for side, d in enumerate((1, -1)):
            slot = at(a_order[k], d * (5 - h))
            if h > 1:
                add(a1, (h - 1, k, d), slot)
            part = A_HALF[side] if h == 1 else A
            send(a1, (h, k, d), slot, part, place.along_z(d), "a")

    def b1_step(i):
        h, k = i // 8 + 1, i % 8
        for side, d in enumerate((1, -1)):
            slot = at(d * (3 - h), b_order[k])
            if h == 2:
                add(b1, (1, k, d), slot)
            part = B_HALF[side] if h == 1 else B
            send(b1, (h, k, d), slot, part, place.along_y(d), "b")

    def a1_end(k):
        for d in (1, -1):
            add(a1, (4, k, d), at(a_order[k], 0))

    def b1_end(k):
        for d in (1, -1):
            add(b1, (2, k, d), at(0, b_order[k]))

    def a2_step(h):
        for side, d in enumerate((1, -1)):
            slot = at(d * (3 - h), 0)
            if h == 2:
                add(a2, (1, d), slot)
            send(a2, (h, d), slot, A_HALF[side] if h == 1 else A, place.along_y(d), "a")

    def b2_step(h):
        for side, d in enumerate((1, -1)):
            slot = at(0, d * (5 - h))
            if h > 1:
                add(b2, (h - 1, d), slot)
            send(b2, (h, d), slot, B_HALF[side] if h == 1 else B, place.along_z(d), "b")

    def end(book, key, part):
        own = at(0, 0)
        for d in (1, -1):
            add(book, key + (d,), own)
        cols(result, own, part)[...] = cols(part_sums, own, part)[...]

    def step(i):
        if i < 16:
            a1_step(i)
            b1_step(i)
        if 0 <= i - 10 < 8:
            b1_end(i - 10)
        if 0 <= i - 14 < 4:
            a1_end(i - 14)
        if i in (10, 12, 14, 16):
            b2_step((i - 8) // 2)
        if i in (14, 16):
            a2_step((i - 12) // 2)
        if i == 18:
            end(a2, (2,), A)
            end(b2, (4,), B)

    return [functools.partial(step, i) for i in range(19)]


A_LANDS = 4 * 4 * 2 + 2 * 2
B_LANDS = 2 * 8 * 2 + 4 * 2
GATHER_WIRES = 4 + 8 + 32 + 32
SCATTER_WIRES = 32 + 32 + 4 + 8
WIRES = 2 * GATHER_WIRES + SCATTER_WIRES + 7 + 7 + 7 + 3 + 7 + 7 + 7


def column_block(c):
    return pl.ds(pl.multiple_of(c * BLOCK, BLOCK), BLOCK)


def core(
    momentum, gradient, basis,
    coeffs, ortho, inverse, new_basis,
    q_all, w_part, w_all, land_a, land_b, m_buf, g_buf, b_high, b_low,
    p_part, p_land, p_all, p_t, gram_own, gram_z, gram_y, work, linv, norms,
    send, recv, local,
):
    place = Place()
    wires = Wires(send, recv)
    f, t, y, z = place.f, place.t, place.y, place.z

    loads = [
        pltpu.make_async_copy(basis, q_all.at[f], local.at[0]),
        pltpu.make_async_copy(momentum, m_buf, local.at[1]),
        pltpu.make_async_copy(gradient, g_buf, local.at[2]),
    ]
    for load in loads:
        load.start()

    barrier = pltpu.get_barrier_semaphore()
    peers = (
        [place.along_y(d) for d in range(1, Y)]
        + [place.along_z(d) for d in range(1, Z)]
        + [place.along_t(d) for d in range(1, T)]
    )
    for peer in peers:
        pl.semaphore_signal(barrier, inc=1, device_id=peer, device_id_type=MESH)
    pl.semaphore_wait(barrier, len(peers))

    loads[0].wait()
    steps = gather_steps(place, wires, q_all)
    for step in steps[:2]:
        step()
    loads[1].wait()
    loads[2].wait()

    @pl.loop(0, N // BLOCK)
    def _(c):
        at = column_block(c)
        high, low = split(m_buf[:, at] + g_buf[:, at].astype(f32))
        b_high[:, at] = high
        b_low[:, at] = low

    for step in steps[2:]:
        step()

    p_part[...] = jnp.zeros_like(p_part)

    @pl.loop(0, N // BLOCK)
    def _(c):
        at = column_block(c)
        q = split(q_all[:, :, at].reshape(RANK, BLOCK))
        p_part[...] += dot3((b_high[:, at], b_low[:, at]), q, ((1,), (1,))).reshape(T, M // T, RANK)

    copies = []
    for d in range(1, T):
        copies.append(wires.start(p_part.at[(t + d) % T], p_land.at[t], place.along_t(d)))
    p_land[t] = p_part[t]
    for copy in copies:
        copy.wait_recv()
    total = p_land[0]
    for i in range(1, T):
        total = total + p_land[i]
    p_all[t] = total
    copies = [wires.start(p_all.at[t], p_all.at[t], place.along_t(d)) for d in range(1, T)]
    for copy in copies:
        copy.wait_recv()

    proj = p_all[...].reshape(M, RANK)
    p_t[...] = proj.T
    rows = p_t[pl.ds(pl.multiple_of(t * (RANK // T), RANK // T), RANK // T), :]
    own = exact(rows, proj)
    for j in range(Z):
        gram_own[j] = own[8 * (j // 2) : 8 * (j // 2) + 8, 128 * (j % 2) : 128 * (j % 2) + 128]
    gram_copies = [
        wires.start(gram_own.at[(z + d) % Z], gram_z.at[z], place.along_z(d)) for d in range(1, Z)
    ]
    gram_sent = list(gram_copies)
    gram_z[z] = gram_own[z]

    pt_split = split(p_t[...])

    @pl.loop(0, N // BLOCK)
    def _(c):
        at = column_block(c)
        w_part[:, :, at] = dot3(pt_split, (b_high[:, at], b_low[:, at])).reshape(F, R, BLOCK)

    def summed(ref, count):
        total = ref[0]
        for i in range(1, count):
            total = total + ref[i]
        return total

    tile = (4 * t + z // 2, slice(None), pl.ds(pl.multiple_of(z % 2 * 128, 128), 128))

    def gram_1():
        for copy in gram_copies:
            copy.wait_recv()
        gram_y[y] = summed(gram_z, Z)
        gram_copies[:] = [
            wires.start(gram_y.at[y], gram_y.at[y], place.along_y(d)) for d in range(1, Y)
        ]

    def gram_2():
        for copy in gram_copies:
            copy.wait_recv()
        work[tile] = summed(gram_y, Y)
        gram_sent.extend(gram_copies)
        gram_copies[:] = [
            wires.start(work.at[tile], work.at[tile], place.along_z(d)) for d in range(1, Z)
        ]

    def gram_3():
        for copy in gram_copies:
            copy.wait_recv()
        own = work.at[pl.ds(4 * t, 4), :, pl.ds(0, RANK)]
        gram_sent.extend(gram_copies)
        gram_copies[:] = [wires.start(own, own, place.along_t(d)) for d in range(1, T)]

    def gram_4():
        for copy in gram_copies:
            copy.wait_recv()
        wires.drain(gram_sent + gram_copies)
        row = lax.broadcasted_iota(jnp.int32, (RANK, RANK), 0)
        lane = lax.broadcasted_iota(jnp.int32, (RANK, RANK), 1)
        work[:, :, RANK:] = jnp.where(row == lane, 1.0, 0.0).astype(f32).reshape(F, R, RANK)

    lane = lax.broadcasted_iota(jnp.int32, (NB, 128), 1)
    sub = lax.broadcasted_iota(jnp.int32, (NB, 128), 0)

    def panel(p):
        tiles = NB // R
        here = work[pl.ds(p * tiles, tiles)].reshape(NB, 2 * RANK)
        first = p * NB
        low_half = jnp.where(first < 128, here[:, :128], here[:, 128:256])
        block = pltpu.roll(low_half, (128 - first % 128) % 128, 1)
        block = jnp.where(lane < NB, block, jnp.where(lane == sub + NB, 1.0, 0.0))
        diag = jnp.ones((NB, 128), f32)
        for j in range(NB):
            pivot = block[j : j + 1, j : j + 1]
            factor = block[:, j : j + 1] * (1.0 / pivot)
            diag = jnp.where(sub == j, pivot, diag)
            if j < NB - 1:
                block = block - jnp.where(sub > j, factor, 0.0) * block[j : j + 1, :]
        inverse_block = (block * lax.rsqrt(diag))[:, NB : 2 * NB]
        done = exact(inverse_block, here)
        linv[pl.ds(p * tiles, tiles)] = done[:, RANK:].reshape(tiles, R, RANK)
        high = done.astype(bf16).astype(f32)
        mid = (done - high).astype(bf16).astype(f32)
        low = (done - high) - mid
        left = jnp.concatenate([x[:, :RANK] for x in (high, high, mid, high, low, mid)]).astype(bf16)
        right = jnp.concatenate([high, mid, high, low, high, mid]).astype(bf16)
        work[...] -= dot(left, right, ((0,), (0,))).reshape(F, R, 2 * RANK)

    def panels(begin, end):
        def run():
            @pl.loop(begin, end)
            def _(p):
                panel(p)

        return run

    count = RANK // NB
    side = [None, gram_1, None, gram_2, None, gram_3, None, gram_4]
    side += [panels(p, p + 1) for p in range(count)]

    steps = scatter_steps(place, wires, w_part, w_all, land_a, land_b)
    steps = steps + gather_steps(place, wires, w_all)
    for step in steps:
        step()
        if side:
            work_beside = side.pop(0)
            if work_beside is not None:
                work_beside()
    for work_beside in side:
        work_beside()

    factor_inverse = split(linv[...].reshape(RANK, RANK))
    ortho[...] = exact(p_all[...].reshape(M, RANK), linv[...].reshape(RANK, RANK), ((1,), (1,)))
    norms[0] = jnp.zeros((RANK, 128), f32)

    @pl.loop(0, N // BLOCK)
    def _(c):
        at = column_block(c)
        part = dot3(factor_inverse, split(w_all[:, :, at].reshape(RANK, BLOCK)))
        coeffs[:, at] = part
        squares = part * part
        norms[0] += squares[:, :128] + squares[:, 128:]

    norms_t = norms[0].T
    own_norms = jnp.sum(norms_t, axis=0, keepdims=True)
    inverse_land = norms.at[1]
    inverse_land[pl.ds(pl.multiple_of(t * 16, 16), 8), :] = jnp.broadcast_to(own_norms[:, :128], (8, 128))
    inverse_land[pl.ds(pl.multiple_of(t * 16, 16) + 8, 8), :] = jnp.broadcast_to(own_norms[:, 128:], (8, 128))
    mine = inverse_land.at[pl.ds(pl.multiple_of(t * 16, 16), 16), :]
    copies = [wires.start(mine, mine, place.along_t(d)) for d in range(1, T)]
    for copy in copies:
        copy.wait_recv()
    total = inverse_land[0:16, :]
    for i in range(1, T):
        total = total + inverse_land[16 * i : 16 * i + 16, :]
    scale = lax.rsqrt(total + norm_eps)
    inverse_row = jnp.concatenate([scale[0:8], scale[8:16]], axis=1)
    inverse[...] = inverse_row
    lanes = lax.broadcasted_iota(jnp.int32, (R, RANK), 1)
    subs = lax.broadcasted_iota(jnp.int32, (R, RANK), 0)
    own_inverse = jnp.sum(jnp.where(lanes == subs + f * R, inverse_row, 0.0), axis=1, keepdims=True)
    new_basis[...] = coeffs[pl.ds(pl.multiple_of(f * R, R), R), :] * own_inverse
    wires.drain()
    assert wires.count == WIRES


def core_call(momentum, gradient, basis):
    any_space = pl.BlockSpec(memory_space=pl.ANY)
    vmem = pl.BlockSpec(memory_space=pltpu.VMEM)
    return pl.pallas_call(
        core,
        out_shape=(
            jax.ShapeDtypeStruct((RANK, N), f32),
            jax.ShapeDtypeStruct((M, RANK), f32),
            jax.ShapeDtypeStruct((8, RANK), f32),
            jax.ShapeDtypeStruct((R, N), f32),
        ),
        in_specs=[any_space] * 3,
        out_specs=(vmem,) * 4,
        scratch_shapes=[
            pltpu.VMEM((F, R, N), f32),
            pltpu.VMEM((F, R, N), f32),
            pltpu.VMEM((F, R, N), f32),
            pltpu.VMEM((A_LANDS, R, A[1]), f32),
            pltpu.VMEM((B_LANDS, R, B[1]), f32),
            pltpu.VMEM((M, N), f32),
            pltpu.VMEM((M, N), bf16),
            pltpu.VMEM((M, N), bf16),
            pltpu.VMEM((M, N), bf16),
            pltpu.VMEM((T, M // T, RANK), f32),
            pltpu.VMEM((T, M // T, RANK), f32),
            pltpu.VMEM((T, M // T, RANK), f32),
            pltpu.VMEM((RANK, M), f32),
            pltpu.VMEM((Z, 8, 128), f32),
            pltpu.VMEM((Z, 8, 128), f32),
            pltpu.VMEM((Y, 8, 128), f32),
            pltpu.VMEM((F, R, 2 * RANK), f32),
            pltpu.VMEM((F, R, RANK), f32),
            pltpu.VMEM((2, RANK, 128), f32),
            pltpu.SemaphoreType.DMA((WIRES,)),
            pltpu.SemaphoreType.DMA((WIRES,)),
            pltpu.SemaphoreType.DMA((3,)),
        ],
        compiler_params=pltpu.CompilerParams(
            collective_id=0, has_side_effects=True, vmem_limit_bytes=56 * 2**20
        ),
        name="core",
    )(momentum, gradient, basis)


def update(momentum, gradient, coeffs, ortho, inverse, new_momentum, step):
    buffer = momentum[...] + gradient[...].astype(f32)
    high, low = split(coeffs[...])
    basis = ortho[...]
    new_momentum[...] = buffer - (1.0 - momentum_decay) * dot(basis.astype(bf16), high)
    scale = (ROWS * COLS / RANK) ** 0.5
    scaled = split(basis * (inverse[0:1, :] * scale))
    step[...] = dot3(scaled, (high, low)).astype(bf16)


def update_call(momentum, gradient, coeffs, ortho, inverse):
    def block(rows):
        return pl.BlockSpec((rows, BLOCK), lambda c: (0, c))

    return pl.pallas_call(
        update,
        grid=(N // BLOCK,),
        out_shape=(jax.ShapeDtypeStruct((M, N), f32), jax.ShapeDtypeStruct((M, N), bf16)),
        in_specs=[
            block(M), block(M), block(RANK),
            pl.BlockSpec((M, RANK), lambda c: (0, 0)),
            pl.BlockSpec((8, RANK), lambda c: (0, 0)),
        ],
        out_specs=(block(M), block(M)),
        name="update",
    )(momentum, gradient, coeffs, ortho, inverse)


def on_device(momentum, gradient, basis):
    coeffs, ortho, inverse, new_basis = core_call(momentum, gradient, basis)
    new_momentum, step = update_call(momentum, gradient, coeffs, ortho, inverse)
    return (new_momentum, new_basis, step)


def solution(mesh):
    placed = (P("fsdp", "tp"), P("fsdp", "tp"), P("fsdp", "tp"))
    return jax.shard_map(
        on_device,
        mesh=mesh,
        in_specs=placed,
        out_specs=(P("fsdp", "tp"), P("fsdp", "tp"), P("fsdp", "tp")),
        check_vma=False,
    )
```

time: 586 us -> 147 us (0.25)
  waiting for transfers between devices: 447 us -> 0 us
  Pallas kernels: 0 us -> 145 us
  other arithmetic: 62.2 us -> 0 us
  matrix products: 33 us -> 0 us
  blocking collectives: 16.4 us -> 0 us
  between operations: 15.2 us -> 0.65 us
  local copies, waits for them, and re-layouts: 11 us -> 0.65 us
    psum x3 -> x0, waiting for transfers between devices: 363 us -> none  [the longest x1 157 us: on_device(): coeffs = lax.psum(mat(ortho_basis.T, buffer), 'fsdp')]
    pallas_call x0 -> x2, Pallas kernels: none -> 145 us  [the longest x1 134 us: core_call(): pl.pallas_call(core, out_shape=(jax.ShapeDtypeStruct((RANK, N), f32), jax...]
    all_gather x1 -> x0, waiting for transfers between devices: 83.5 us -> none  [on_device(): lax.all_gather(basis, 'fsdp', axis=0, tiled=True)]
    another operation x9 -> x0, other arithmetic: 58 us -> none  [the longest x6 35.2 us: orthogonal(): factor = jnp.linalg.cholesky(gram_matrix)]
    dot_general x5 -> x0, matrix products: 26.5 us -> none  [mat(): jnp.dot(left, right, precision=lax.Precision.HIGHEST, preferred_element_t...]
    psum x1 -> x0, blocking collectives: 16.4 us -> none  [on_device(): squares = lax.psum(jnp.sum(coeffs * coeffs, axis=1), 'tp')]
    another operation x9 -> x0, local copies, waits for them, and re-layouts: 7.74 us -> none
    another operation x5 -> x0, matrix products: 6.51 us -> none  [the longest x3 3.71 us: orthogonal(): lax.linalg.triangular_solve(factor, projected, left_side=False, lower=Tru...]
  transfers between devices with their start and end apart: 4 -> 0, of which waited for: 4 -> 0; matrix products, arithmetic and copies ran while one was open for 0% -> 0% of each run, Pallas kernels for 0% -> 0%
where the time goes in v1:
time: 147 us; the launch traced here: 146 us
  Pallas kernels  145 us (99%)
    pallas_call x1, Pallas kernels, core_call(): pl.pallas_call(core, out_shape=(jax.ShapeDtypeStruct((RANK, N), f32), jax...  134 us
    pallas_call x1, Pallas kernels, update_call(): pl.pallas_call(update, grid=(N // BLOCK,), out_shape=(jax.ShapeDtypeStruc...  11.4 us

profile of v1, /device:TPU:1, one launch (start us, length us, event | category | flops | bytes accessed | tf_op | source)
XLA Modules:
  0.0 146.3 jit_solution(3270979492052100894)
XLA Ops:
  0.6 133.6 %core.1 = (f32[256,3328]{1,0:T(8,128)}, f32[256,256]{1,0:T(8,128)}, f32[8,256]{1,0:T(8,128)}, f32[8,3328]{1,0:T(8,128)}) custom-call(f32[256,3328]{1,0:T(8,128)} %momentum.3, bf16[256,3328]{1,0:T(8,128)(2,1)} %gradient.3, f32[8,3328]{1,0:T(8,128)} %basis.1), custom_call_target="tpu_custom_call" | custom-call | tf_op jit(solution)/shard_map/core/pallas_call | solution.py:481
  134.2 0.0 copy-start
  134.3 11.4 %update.1 = (f32[256,3328]{1,0:T(8,128)}, bf16[256,3328]{1,0:T(8,128)(2,1)}) custom-call(f32[256,3328]{1,0:T(8,128)} %momentum.3, bf16[256,3328]{1,0:T(8,128)(2,1)} %gradient.3, f32[256,3328]{1,0:T(8,128)} %get-tuple-element.9.coeffs, f32[256,256]{1,0:T(8,128)} %get-tuple-element.10.ortho, f32[8,256]{1,0:T(8,128)} %get-tuple-element.11.inverse), custom_call_target="tpu_custom_call" | custom-call | tf_op jit(solution)/shard_map/update/pallas_call | solution.py:536
  145.6 0.0 copy-done
  145.6 0.6 copy.7
Async XLA Ops:
  134.2 11.4 %copy-start = (f32[8,3328]{1,0:T(8,128)S(1)}, f32[8,3328]{1,0:T(8,128)}, u32[]{:S(2)}) copy-start(f32[8,3328]{1,0:T(8,128)} %get-tuple-element.19) | copy-start | bytes 319492

commit v2 on v1

v2 whole, which is shorter than its diff:
```python
import functools

import jax
import jax.numpy as jnp
from jax import lax
from jax.experimental import pallas as pl
from jax.experimental.pallas import tpu as pltpu
from jax.sharding import PartitionSpec as P

ROWS = 8192
COLS = 26624
RANK = 256

momentum_decay = 0.95
norm_eps = 1e-06

Y, Z, T = 4, 8, 8
F = Y * Z
M = ROWS // F
N = COLS // T
R = RANK // F
BLOCK = 256
NB = 16


class Part:
    def __init__(self, begin, size, cut):
        self.begin, self.size = begin, size
        self.a, self.b = (begin, cut), (begin + cut, size - cut)
        self.a_half, self.b_half = self.halves(self.a), self.halves(self.b)

    @staticmethod
    def halves(part):
        first = (part[1] // 128 + 1) // 2 * 128
        return (part[0], first), (part[0] + first, part[1] - first)


PART = Part(0, N, 1408)
A_LANDS = 4 * 4 * 2 + 2 * 2
B_LANDS = 2 * 8 * 2 + 4 * 2
POOL = 40
SHIFT = 2

MESH = pl.DeviceIdType.MESH
f32, bf16 = jnp.float32, jnp.bfloat16


def split(value):
    high = value.astype(bf16)
    return high, (value - high.astype(f32)).astype(bf16)


def dot(left, right, dims=((1,), (0,))):
    return lax.dot_general(left, right, (dims, ((), ())), preferred_element_type=f32)


def dot3(left, right, dims=((1,), (0,))):
    (lh, ll), (rh, rl) = left, right
    return dot(lh, rh, dims) + (dot(lh, rl, dims) + dot(ll, rh, dims))


def exact(left, right, dims=((1,), (0,))):
    return lax.dot_general(
        left, right, (dims, ((), ())), precision=lax.Precision.HIGHEST, preferred_element_type=f32
    )


class Wires:
    def __init__(self, send, recv):
        self.send, self.recv = send, recv
        self.sent, self.used = {}, 0

    def range(self, begin, count):
        indices = iter(range(begin, begin + count))
        return lambda src, dst, to: self.start(src, dst, to, next(indices))

    def start(self, src, dst, to, index):
        place = self.used % POOL
        self.wait_sent(self.sent.get(place))
        copy = pltpu.make_async_remote_copy(
            src_ref=src,
            dst_ref=dst,
            send_sem=self.send.at[place],
            recv_sem=self.recv.at[index],
            device_id=to,
            device_id_type=MESH,
        )
        copy.start()
        self.sent[place] = copy
        self.used += 1
        return copy

    def wait_sent(self, copy):
        for place, other in list(self.sent.items()):
            if other is copy:
                copy.wait_send()
                del self.sent[place]

    def drain(self, copies=None):
        for copy in list(self.sent.values()) if copies is None else copies:
            self.wait_sent(copy)


class Place:
    def __init__(self):
        self.f = lax.axis_index("fsdp")
        self.t = lax.axis_index("tp")
        self.y, self.z = self.f // Z, self.f % Z
        self.x, self.c = self.t // 2, self.t % 2

    def slot(self, dy, dz):
        return (self.y + dy + Y) % Y * Z + (self.z + dz + Z) % Z

    def along_y(self, d):
        return {"fsdp": self.slot(d, 0)}

    def along_z(self, d):
        return {"fsdp": self.slot(0, d)}

    def along_x(self, d):
        return {"tp": (self.x + d) % 4 * 2 + self.c}

    def other_core(self):
        return {"tp": self.x * 2 + 1 - self.c}


def cols(ref, slot, part):
    return ref.at[slot, :, pl.ds(part[0], part[1])]


def gather_steps(place, start, buf, part):
    a1, b1, a2, b2 = {}, {}, {}, {}
    a_order = (0, -1, 1, 2)
    b_order = (0, -1, 1, -2, 2, -3, 3, 4)
    at = place.slot

    def send(book, key, slot, piece, to):
        book[key] = start(cols(buf, slot, piece), cols(buf, slot, piece), to)

    def a2_step(i):
        h, k = i // 4 + 1, i % 4
        for side, d in enumerate((1, -1)):
            if h > 1:
                a2[h - 1, k, d].wait_recv()
            piece = part.a_half[side] if h == 4 else part.a
            send(a2, (h, k, d), at(a_order[k], -d * (h - 1)), piece, place.along_z(d))

    def b2_step(i):
        h, k = i // 8 + 1, i % 8
        for side, d in enumerate((1, -1)):
            if h == 2:
                b2[1, k, d].wait_recv()
            piece = part.b_half[side] if h == 2 else part.b
            send(b2, (h, k, d), at(-d * (h - 1), b_order[k]), piece, place.along_y(d))

    def a1_step(i):
        if i == 0:
            for d in (1, -1):
                send(a1, (1, d), at(0, 0), part.a, place.along_y(d))
        elif i in (1, 2):
            side, d = i - 1, (1, -1)[i - 1]
            a1[1, d].wait_recv()
            send(a1, (2, d), at(-d, 0), part.a_half[side], place.along_y(d))
        elif i == 3:
            for d in (1, -1):
                a1[2, d].wait_recv()

    def b1_step(i):
        if i == 0:
            for d in (1, -1):
                send(b1, (1, d), at(0, 0), part.b, place.along_z(d))
        elif i in range(1, 7):
            h, side = (i + 1) // 2, (i + 1) % 2
            d = (1, -1)[side]
            b1[h, d].wait_recv()
            piece = part.b_half[side] if h == 3 else part.b
            send(b1, (h + 1, d), at(0, -d * h), piece, place.along_z(d))
        elif i == 7:
            for d in (1, -1):
                b1[4, d].wait_recv()

    def step(i):
        b1_step(i)
        a1_step(i)
        b2_step(i)
        a2_step(i)

    def last():
        for k in range(4):
            for d in (1, -1):
                a2[4, k, d].wait_recv()
        for k in range(8):
            for d in (1, -1):
                b2[2, k, d].wait_recv()

    return [functools.partial(step, i) for i in range(16)] + [last]


def scatter_steps(place, start, part_sums, result, land_a, land_b, part):
    a1, b1, a2, b2 = {}, {}, {}, {}
    a_order = (2, 1, -1, 0)
    b_order = (4, 3, -3, 2, -2, 1, -1, 0)
    at = place.slot
    used = {"a": 0, "b": 0}

    def send(book, key, slot, piece, to, kind):
        land = land_a if kind == "a" else land_b
        index, offset = used[kind], piece[0] - (part.a if kind == "a" else part.b)[0]
        used[kind] += 1
        target = land.at[index, :, pl.ds(offset, piece[1])]
        book[key] = (start(cols(part_sums, slot, piece), target, to), target, piece)

    def add(book, key, slot):
        copy, target, piece = book[key]
        copy.wait_recv()
        own = cols(part_sums, slot, piece)
        own[...] += target[...]

    def a1_step(i):
        h, k = i // 4 + 1, i % 4
        for side, d in enumerate((1, -1)):
            slot = at(a_order[k], d * (5 - h))
            if h > 1:
                add(a1, (h - 1, k, d), slot)
            piece = part.a_half[side] if h == 1 else part.a
            send(a1, (h, k, d), slot, piece, place.along_z(d), "a")

    def b1_step(i):
        h, k = i // 8 + 1, i % 8
        for side, d in enumerate((1, -1)):
            slot = at(d * (3 - h), b_order[k])
            if h == 2:
                add(b1, (1, k, d), slot)
            piece = part.b_half[side] if h == 1 else part.b
            send(b1, (h, k, d), slot, piece, place.along_y(d), "b")

    def a1_end(k):
        for d in (1, -1):
            add(a1, (4, k, d), at(a_order[k], 0))

    def b1_end(k):
        for d in (1, -1):
            add(b1, (2, k, d), at(0, b_order[k]))

    def a2_step(h):
        for side, d in enumerate((1, -1)):
            slot = at(d * (3 - h), 0)
            if h == 2:
                add(a2, (1, d), slot)
            send(a2, (h, d), slot, part.a_half[side] if h == 1 else part.a, place.along_y(d), "a")

    def b2_step(h):
        for side, d in enumerate((1, -1)):
            slot = at(0, d * (5 - h))
            if h > 1:
                add(b2, (h - 1, d), slot)
            send(b2, (h, d), slot, part.b_half[side] if h == 1 else part.b, place.along_z(d), "b")

    def end(book, key, piece):
        own = at(0, 0)
        for d in (1, -1):
            add(book, key + (d,), own)
        cols(result, own, piece)[...] = cols(part_sums, own, piece)[...]

    def step(i):
        if i < 16:
            a1_step(i)
        if 0 <= i - SHIFT < 16:
            b1_step(i - SHIFT)
        if 0 <= i - SHIFT - 10 < 8:
            b1_end(i - SHIFT - 10)
        if 0 <= i - 14 < 4:
            a1_end(i - 14)
        if i - SHIFT in (10, 12, 14, 16):
            b2_step((i - SHIFT - 8) // 2)
        if i in (14, 16):
            a2_step((i - 12) // 2)
        if i == 18:
            end(a2, (2,), part.a)
        if i - SHIFT == 18:
            end(b2, (4,), part.b)

    return [functools.partial(step, i) for i in range(19 + SHIFT)]


GATHER_WIRES = 4 + 8 + 32 + 32
SCATTER_WIRES = 32 + 32 + 4 + 8
OTHER_WIRES = 11 + 24 + 4
WIRES = GATHER_WIRES + SCATTER_WIRES + OTHER_WIRES


def column_block(c):
    return pl.ds(pl.multiple_of(c * BLOCK, BLOCK), BLOCK)


def block_pieces(body, begin, end, size):
    def piece(first, last):
        def run():
            @pl.loop(first, last)
            def _(c):
                body(column_block(c))

        return run

    return [piece(c, min(c + size, end)) for c in range(begin, end, size)]


def in_order(timed):
    for _, _, step in sorted((key, n, step) for n, (key, step) in enumerate(timed)):
        step()


def at_times(steps, begin, apart=1.0):
    return [(begin + apart * i, step) for i, step in enumerate(steps)]


def core(
    momentum, gradient, basis,
    coeffs, ortho, inverse, new_basis,
    q_all, w_part, w_all, land_a, land_b, m_buf, g_buf, b_high, b_low, c_buf,
    p_part, p_core, p_x, p_all, p_t, gram_own, gram_z, gram_y, work, linv, linv_high, linv_low, norm_sum, norm_core, norm_x,
    send, recv, local,
):
    place = Place()
    wires = Wires(send, recv)
    start = wires.range(GATHER_WIRES + SCATTER_WIRES, OTHER_WIRES)
    f, t, y, z, x, core_index = place.f, place.t, place.y, place.z, place.x, place.c

    loads = [
        pltpu.make_async_copy(basis, q_all.at[f], local.at[0]),
        pltpu.make_async_copy(momentum, m_buf, local.at[1]),
        pltpu.make_async_copy(gradient, g_buf, local.at[2]),
    ]
    for load in loads:
        load.start()

    barrier = pltpu.get_barrier_semaphore()
    peers = (
        [place.along_y(d) for d in range(1, Y)]
        + [place.along_z(d) for d in range(1, Z)]
        + [place.along_x(d) for d in range(1, 4)]
        + [place.other_core()]
    )
    for peer in peers:
        pl.semaphore_signal(barrier, inc=1, device_id=peer, device_id_type=MESH)
    pl.semaphore_wait(barrier, len(peers))

    def split_block(at):
        high, low = split(m_buf[:, at] + g_buf[:, at].astype(f32))
        b_high[:, at] = high
        b_low[:, at] = low

    def project(at):
        q = split(q_all[:, :, at].reshape(RANK, BLOCK))
        p_part[...] += dot3((b_high[:, at], b_low[:, at]), q, ((1,), (1,))).reshape(T, M // T, RANK)

    def loaded():
        p_part[...] = jnp.zeros_like(p_part)
        loads[1].wait()
        loads[2].wait()

    blocks = N // BLOCK
    loads[0].wait()
    timed = at_times(gather_steps(place, wires.range(0, GATHER_WIRES), q_all, PART), 0)
    timed += [(1.4, loaded)]
    timed += at_times(block_pieces(split_block, 0, blocks, 1), 1.5)
    in_order(timed)
    for piece in block_pieces(project, 0, blocks, blocks):
        piece()

    mine = 4 * core_index
    copy = start(p_part.at[pl.ds(4 - mine, 4)], p_core, place.other_core())
    copy.wait_recv()
    p_core[...] += p_part[pl.ds(mine, 4)]
    copies = [
        start(p_core.at[(x + d) % 4], p_x.at[x], place.along_x(d)) for d in (2, 1, 3)
    ]
    p_x[x] = p_core[x]
    for copy in copies:
        copy.wait_recv()
    p_all[mine + x] = (p_x[0] + p_x[1]) + (p_x[2] + p_x[3])

    def copy_p(block, to):
        return start(p_all.at[block], p_all.at[block], to)

    copies = [copy_p(mine + x, place.along_x(d)) for d in (2, 1, 3)]
    core_copies = [copy_p(mine + x, place.other_core())]
    for d, copy in ((1, copies[1]), (3, copies[2]), (2, copies[0])):
        copy.wait_recv()
        core_copies.append(copy_p(mine + (x - d + 4) % 4, place.other_core()))
    for copy in core_copies:
        copy.wait_recv()

    proj = p_all[...].reshape(M, RANK)
    p_t[...] = proj.T
    rows = p_t[pl.ds(pl.multiple_of(t * (RANK // T), RANK // T), RANK // T), :]
    own = exact(rows, proj)
    for j in range(Z):
        gram_own[j] = own[8 * (j // 2) : 8 * (j // 2) + 8, 128 * (j % 2) : 128 * (j % 2) + 128]
    gram_copies = [
        start(gram_own.at[(z + d) % Z], gram_z.at[z], place.along_z(d)) for d in range(1, Z)
    ]
    gram_sent = list(gram_copies)
    gram_z[z] = gram_own[z]

    pt_split = split(p_t[...])

    def coefficients(at):
        w_part[:, :, at] = dot3(pt_split, (b_high[:, at], b_low[:, at])).reshape(F, R, BLOCK)

    a_blocks = -(-PART.a[1] // BLOCK)
    for piece in block_pieces(coefficients, 0, a_blocks, a_blocks):
        piece()

    def summed(ref, count):
        total = ref[0]
        for i in range(1, count):
            total = total + ref[i]
        return total

    def arrived(*sent):
        for copy in gram_copies:
            copy.wait_recv()
        gram_copies.clear()

    def send_gram(copies):
        gram_copies.extend(copies)
        gram_sent.extend(copies)

    tile = (4 * t + z // 2, slice(None), pl.ds(pl.multiple_of(z % 2 * 128, 128), 128))

    def gram_rows(owner):
        return work.at[pl.ds(4 * owner, 4), :, pl.ds(0, RANK)]

    def to_other_core(owner):
        return start(gram_rows(owner), gram_rows(owner), place.other_core())

    def gram_1():
        arrived()
        gram_y[y] = summed(gram_z, Z)
        send_gram([start(gram_y.at[y], gram_y.at[y], place.along_y(d)) for d in range(1, Y)])

    def gram_2():
        arrived()
        work[tile] = summed(gram_y, Y)
        send_gram([start(work.at[tile], work.at[tile], place.along_z(d)) for d in range(1, Z)])

    def gram_3():
        arrived()
        send_gram([start(gram_rows(t), gram_rows(t), place.along_x(d)) for d in range(1, 4)])

    def gram_4():
        arrived()
        send_gram([to_other_core((x + d) % 4 * 2 + core_index) for d in range(4)])

    def gram_5():
        arrived()
        wires.drain(gram_sent)
        row = lax.broadcasted_iota(jnp.int32, (RANK, RANK), 0)
        lane = lax.broadcasted_iota(jnp.int32, (RANK, RANK), 1)
        work[:, :, RANK:] = jnp.where(row == lane, 1.0, 0.0).astype(f32).reshape(F, R, RANK)

    lane = lax.broadcasted_iota(jnp.int32, (NB, 128), 1)
    sub = lax.broadcasted_iota(jnp.int32, (NB, 128), 0)

    def panel(p):
        tiles = NB // R
        here = work[pl.ds(p * tiles, tiles)].reshape(NB, 2 * RANK)
        start = p * NB
        low_half = jnp.where(start < 128, here[:, :128], here[:, 128:256])
        block = pltpu.roll(low_half, (128 - start % 128) % 128, 1)
        columns = [jnp.broadcast_to(block[:, j : j + 1], (NB, 128)) for j in range(NB)]
        right = jnp.where(lane == sub, 1.0, 0.0).astype(f32)
        diag = jnp.ones((NB, 128), f32)
        for j in range(NB):
            pivot = jnp.broadcast_to(columns[j][j : j + 1, :], (NB, 128))
            diag = jnp.where(sub == j, pivot, diag)
            if j < NB - 1:
                factor = jnp.where(sub > j, columns[j] * (1.0 / pivot), 0.0)
                for i in range(j + 1, NB):
                    columns[i] = columns[i] - factor * columns[i][j : j + 1, :]
                right = right - factor * right[j : j + 1, :]
        right = right * lax.rsqrt(diag)
        done = right[:, 0:1] * here[0:1, :]
        for j in range(1, NB):
            done = done + right[:, j : j + 1] * here[j : j + 1, :]
        linv[pl.ds(p * tiles, tiles)] = done[:, RANK:].reshape(tiles, R, RANK)
        high = done.astype(bf16).astype(f32)
        mid = (done - high).astype(bf16).astype(f32)
        low = (done - high) - mid
        left = jnp.concatenate([v[:, :RANK] for v in (high, high, mid, high, low, mid)]).astype(bf16)
        beside = jnp.concatenate([high, mid, high, low, high, mid]).astype(bf16)
        work[...] -= dot(left, beside, ((0,), (0,))).reshape(F, R, 2 * RANK)

    def panels(begin, end):
        def run():
            @pl.loop(begin, end)
            def _(p):
                panel(p)

        return run

    def orthogonal():
        ortho[...] = exact(p_all[...].reshape(M, RANK), linv[...].reshape(RANK, RANK), ((1,), (1,)))
        linv_high[...], linv_low[...] = split(linv[...].reshape(RANK, RANK))
        norm_sum[...] = jnp.zeros_like(norm_sum)

    def multiply(at):
        part = dot3((linv_high[...], linv_low[...]), split(w_all[:, :, at].reshape(RANK, BLOCK)))
        c_buf[:, at] = part
        squares = part * part
        norm_sum[...] += squares[:, :128] + squares[:, 128:]

    lanes = wires.range(GATHER_WIRES, SCATTER_WIRES)
    steps = scatter_steps(place, lanes, w_part, w_all, land_a, land_b, PART)
    steps += gather_steps(place, wires.range(0, GATHER_WIRES), w_all, PART)
    timed = at_times(steps, 0)
    timed += at_times(block_pieces(coefficients, a_blocks, blocks, blocks), SHIFT - 0.9)
    timed += [(4.5, gram_1), (7.5, gram_2), (11.5, gram_3), (14.5, gram_4), (16.5, gram_5)]
    timed += at_times([panels(p, p + 2) for p in range(0, RANK // NB, 2)], 17.5)
    timed += [(26.5, orthogonal)]
    in_order(timed)

    stores = []
    for size, piece in zip((7, 6), block_pieces(multiply, 0, blocks, 7), strict=True):
        piece()
        at = pl.ds(len(stores) * 7 * BLOCK, size * BLOCK)
        stores.append(pltpu.make_async_copy(c_buf.at[:, at], coeffs.at[:, at], local.at[len(stores)]))
        stores[-1].start()
    own_norms = jnp.sum(norm_sum[...].T, axis=0, keepdims=True)
    norm_core[0, 0:8] = jnp.broadcast_to(own_norms[:, :128], (8, 128))
    norm_core[0, 8:16] = jnp.broadcast_to(own_norms[:, 128:], (8, 128))
    copy = start(norm_core.at[0], norm_core.at[1], place.other_core())
    copy.wait_recv()
    norm_x[x] = norm_core[0] + norm_core[1]
    copies = [start(norm_x.at[x], norm_x.at[x], place.along_x(d)) for d in (2, 1, 3)]
    for copy in copies:
        copy.wait_recv()
    scale = lax.rsqrt((norm_x[0] + norm_x[1]) + (norm_x[2] + norm_x[3]) + norm_eps)
    inverse_row = jnp.concatenate([scale[0:8], scale[8:16]], axis=1)
    inverse[...] = inverse_row
    lanes = lax.broadcasted_iota(jnp.int32, (R, RANK), 1)
    subs = lax.broadcasted_iota(jnp.int32, (R, RANK), 0)
    own_inverse = jnp.sum(jnp.where(lanes == subs + f * R, inverse_row, 0.0), axis=1, keepdims=True)
    new_basis[...] = c_buf[pl.ds(pl.multiple_of(f * R, R), R), :] * own_inverse
    for copy in stores:
        copy.wait()
    wires.drain()


def core_call(momentum, gradient, basis):
    any_space = pl.BlockSpec(memory_space=pl.ANY)
    vmem = pl.BlockSpec(memory_space=pltpu.VMEM)
    return pl.pallas_call(
        core,
        out_shape=(
            jax.ShapeDtypeStruct((RANK, N), f32),
            jax.ShapeDtypeStruct((M, RANK), f32),
            jax.ShapeDtypeStruct((8, RANK), f32),
            jax.ShapeDtypeStruct((R, N), f32),
        ),
        in_specs=[any_space] * 3,
        out_specs=(any_space, vmem, vmem, vmem),
        scratch_shapes=[
            pltpu.VMEM((F, R, N), f32),
            pltpu.VMEM((F, R, N), f32),
            pltpu.VMEM((F, R, N), f32),
            pltpu.VMEM((A_LANDS, R, PART.a[1]), f32),
            pltpu.VMEM((B_LANDS, R, PART.b[1]), f32),
            pltpu.VMEM((M, N), f32),
            pltpu.VMEM((M, N), bf16),
            pltpu.VMEM((M, N), bf16),
            pltpu.VMEM((M, N), bf16),
            pltpu.VMEM((RANK, N), f32),
            pltpu.VMEM((T, M // T, RANK), f32),
            pltpu.VMEM((T // 2, M // T, RANK), f32),
            pltpu.VMEM((T // 2, M // T, RANK), f32),
            pltpu.VMEM((T, M // T, RANK), f32),
            pltpu.VMEM((RANK, M), f32),
            pltpu.VMEM((Z, 8, 128), f32),
            pltpu.VMEM((Z, 8, 128), f32),
            pltpu.VMEM((Y, 8, 128), f32),
            pltpu.VMEM((F, R, 2 * RANK), f32),
            pltpu.VMEM((F, R, RANK), f32),
            pltpu.VMEM((RANK, RANK), bf16),
            pltpu.VMEM((RANK, RANK), bf16),
            pltpu.VMEM((RANK, 128), f32),
            pltpu.VMEM((2, 16, 128), f32),
            pltpu.VMEM((4, 16, 128), f32),
            pltpu.SemaphoreType.DMA((POOL,)),
            pltpu.SemaphoreType.DMA((WIRES,)),
            pltpu.SemaphoreType.DMA((3,)),
        ],
        compiler_params=pltpu.CompilerParams(
            collective_id=0, has_side_effects=True, vmem_limit_bytes=60 * 2**20
        ),
        name="core",
    )(momentum, gradient, basis)


def update(momentum, gradient, coeffs, ortho, inverse, new_momentum, step):
    buffer = momentum[...] + gradient[...].astype(f32)
    high, low = split(coeffs[...])
    basis = ortho[...]
    new_momentum[...] = buffer - (1.0 - momentum_decay) * dot(basis.astype(bf16), high)
    scale = (ROWS * COLS / RANK) ** 0.5
    scaled = split(basis * (inverse[0:1, :] * scale))
    step[...] = dot3(scaled, (high, low)).astype(bf16)


def update_call(momentum, gradient, coeffs, ortho, inverse):
    wide = N // 2

    def block(rows):
        return pl.BlockSpec((rows, wide), lambda c: (0, c))

    return pl.pallas_call(
        update,
        grid=(N // wide,),
        out_shape=(jax.ShapeDtypeStruct((M, N), f32), jax.ShapeDtypeStruct((M, N), bf16)),
        in_specs=[
            block(M), block(M), block(RANK),
            pl.BlockSpec((M, RANK), lambda c: (0, 0)),
            pl.BlockSpec((8, RANK), lambda c: (0, 0)),
        ],
        out_specs=(block(M), block(M)),
        compiler_params=pltpu.CompilerParams(vmem_limit_bytes=60 * 2**20),
        name="update",
    )(momentum, gradient, coeffs, ortho, inverse)


def on_device(momentum, gradient, basis):
    coeffs, ortho, inverse, new_basis = core_call(momentum, gradient, basis)
    new_momentum, step = update_call(momentum, gradient, coeffs, ortho, inverse)
    return (new_momentum, new_basis, step)


def solution(mesh):
    placed = (P("fsdp", "tp"), P("fsdp", "tp"), P("fsdp", "tp"))
    return jax.shard_map(
        on_device,
        mesh=mesh,
        in_specs=placed,
        out_specs=(P("fsdp", "tp"), P("fsdp", "tp"), P("fsdp", "tp")),
        check_vma=False,
    )
```

time: 147 us -> 126 us (0.86)
  Pallas kernels: 145 us -> 125 us
    pallas_call x1, Pallas kernels: 134 us -> 119 us  [core_call(): pl.pallas_call(core, out_shape=(jax.ShapeDtypeStruct((RANK, N), f32), jax...]
    pallas_call x1, Pallas kernels: 11.4 us -> 5.85 us  [update_call(): pl.pallas_call(update, grid=(N // wide,), out_shape=(jax.ShapeDtypeStruct...]
where the time goes in v2:
time: 126 us
  Pallas kernels  125 us (99%)
    pallas_call x1, Pallas kernels, core_call(): pl.pallas_call(core, out_shape=(jax.ShapeDtypeStruct((RANK, N), f32), jax...  119 us
    pallas_call x1, Pallas kernels, update_call(): pl.pallas_call(update, grid=(N // wide,), out_shape=(jax.ShapeDtypeStruct...  5.85 us

profile of v2, /device:TPU:1, one launch (start us, length us, event | category | flops | bytes accessed | tf_op | source)
XLA Modules:
  0.0 126.3 jit_solution(14672227028490810773)
XLA Ops:
  0.6 119.2 %core.1 = (f32[256,3328]{1,0:T(8,128)}, f32[256,256]{1,0:T(8,128)}, f32[8,256]{1,0:T(8,128)}, f32[8,3328]{1,0:T(8,128)}) custom-call(f32[256,3328]{1,0:T(8,128)} %momentum.3, bf16[256,3328]{1,0:T(8,128)(2,1)} %gradient.3, f32[8,3328]{1,0:T(8,128)} %basis.1), custom_call_target="tpu_custom_call" | custom-call | tf_op jit(solution)/shard_map/core/pallas_call | solution.py:554
  119.8 0.0 copy-start
  119.8 5.8 %update.1 = (f32[256,3328]{1,0:T(8,128)}, bf16[256,3328]{1,0:T(8,128)(2,1)}) custom-call(f32[256,3328]{1,0:T(8,128)} %momentum.3, bf16[256,3328]{1,0:T(8,128)(2,1)} %gradient.3, f32[256,3328]{1,0:T(8,128)} %get-tuple-element.9.coeffs, f32[256,256]{1,0:T(8,128)} %get-tuple-element.10.ortho, f32[8,256]{1,0:T(8,128)} %get-tuple-element.11.inverse), custom_call_target="tpu_custom_call" | custom-call | tf_op jit(solution)/shard_map/update/pallas_call | solution.py:617
  125.7 0.0 copy-done
  125.7 0.6 copy.7
Async XLA Ops:
  119.8 5.9 %copy-start = (f32[8,3328]{1,0:T(8,128)S(1)}, f32[8,3328]{1,0:T(8,128)}, u32[]{:S(2)}) copy-start(f32[8,3328]{1,0:T(8,128)} %get-tuple-element.19) | copy-start | bytes 319492

commit v3 on v2

--- a/solution.py
+++ b/solution.py
@@ -35,11 +35,12 @@
         return (part[0], first), (part[0] + first, part[1] - first)
 
 
-PART = Part(0, N, 1408)
+PARTS = (Part(0, N, 2432), Part(0, N, 0))
 A_LANDS = 4 * 4 * 2 + 2 * 2
 B_LANDS = 2 * 8 * 2 + 4 * 2
-POOL = 40
-SHIFT = 2
+POOL = 32
+OTHER_POOL = 16
+EARLY = 7
 
 MESH = pl.DeviceIdType.MESH
 f32, bf16 = jnp.float32, jnp.bfloat16
@@ -65,40 +66,53 @@
     )
 
 
+class Copy:
+    def __init__(self, make):
+        self.make, self.sent = make, False
+
+    def start(self):
+        self.make().start()
+
+    def wait_recv(self):
+        self.make().wait_recv()
+
+    def wait_send(self):
+        if not self.sent:
+            self.make().wait_send()
+        self.sent = True
+
+
 class Wires:
-    def __init__(self, send, recv):
-        self.send, self.recv = send, recv
-        self.sent, self.used = {}, 0
+    def __init__(self, send, recv, first, size):
+        self.send, self.recv, self.first, self.size = send, recv, first, size
+        self.last, self.used = {}, 0
 
     def range(self, begin, count):
         indices = iter(range(begin, begin + count))
         return lambda src, dst, to: self.start(src, dst, to, next(indices))
 
     def start(self, src, dst, to, index):
-        place = self.used % POOL
-        self.wait_sent(self.sent.get(place))
-        copy = pltpu.make_async_remote_copy(
-            src_ref=src,
-            dst_ref=dst,
-            send_sem=self.send.at[place],
-            recv_sem=self.recv.at[index],
-            device_id=to,
-            device_id_type=MESH,
+        place = self.first + self.used % self.size
+        self.used += 1
+        if place in self.last:
+            self.last[place].wait_send()
+        copy = Copy(
+            lambda: pltpu.make_async_remote_copy(
+                src_ref=src(),
+                dst_ref=dst(),
+                send_sem=self.send.at[place],
+                recv_sem=self.recv.at[index],
+                device_id=to,
+                device_id_type=MESH,
+            )
         )
         copy.start()
-        self.sent[place] = copy
-        self.used += 1
+        self.last[place] = copy
         return copy
 
-    def wait_sent(self, copy):
-        for place, other in list(self.sent.items()):
-            if other is copy:
-                copy.wait_send()
-                del self.sent[place]
-
-    def drain(self, copies=None):
-        for copy in list(self.sent.values()) if copies is None else copies:
-            self.wait_sent(copy)
+    def drain(self):
+        for copy in self.last.values():
+            copy.wait_send()
 
 
 class Place:
@@ -107,9 +121,12 @@
         self.t = lax.axis_index("tp")
         self.y, self.z = self.f // Z, self.f % Z
         self.x, self.c = self.t // 2, self.t % 2
+        self.slots = {
+            (dy, dz): (self.y + dy) % Y * Z + (self.z + dz) % Z for dy in range(Y) for dz in range(Z)
+        }
 
     def slot(self, dy, dz):
-        return (self.y + dy + Y) % Y * Z + (self.z + dz + Z) % Z
+        return self.slots[dy % Y, dz % Z]
 
     def along_y(self, d):
         return {"fsdp": self.slot(d, 0)}
@@ -128,163 +145,187 @@
     return ref.at[slot, :, pl.ds(part[0], part[1])]
 
 
+SIDES = ((0, 1), (1, -1))
+A_ORDER = [(h, k) for h in range(1, 5) for k in range(4)]
+
+
 def gather_steps(place, start, buf, part):
     a1, b1, a2, b2 = {}, {}, {}, {}
-    a_order = (0, -1, 1, 2)
-    b_order = (0, -1, 1, -2, 2, -3, 3, 4)
+    a_slots = (0, -1, 1, 2)
+    b_slots = (0, -1, 1, -2, 2, -3, 3, 4)
+    b_order = [(1, k) for k in range(5)]
+    b_order += [(2, 0), (1, 5), (2, 1), (1, 6), (2, 2), (1, 7)] + [(2, k) for k in range(3, 8)]
     at = place.slot
 
     def send(book, key, slot, piece, to):
-        book[key] = start(cols(buf, slot, piece), cols(buf, slot, piece), to)
-
-    def a2_step(i):
-        h, k = i // 4 + 1, i % 4
-        for side, d in enumerate((1, -1)):
+        def here():
+            return cols(buf, slot, piece)
+
+        book[key] = start(here, here, to)
+
+    def a1_step(k):
+        if k == 0:
+            for d in (2, 1, -1):
+                send(a1, d, at(0, 0), part.a, place.along_y(d))
+        else:
+            a1[-a_slots[k] if k < 3 else 2].wait_recv()
+
+    def a2_step(h, k):
+        for side, d in SIDES:
             if h > 1:
                 a2[h - 1, k, d].wait_recv()
             piece = part.a_half[side] if h == 4 else part.a
-            send(a2, (h, k, d), at(a_order[k], -d * (h - 1)), piece, place.along_z(d))
-
-    def b2_step(i):
-        h, k = i // 8 + 1, i % 8
-        for side, d in enumerate((1, -1)):
+            send(a2, (h, k, d), at(a_slots[k], -d * (h - 1)), piece, place.along_z(d))
+
+    def b1_step(k):
+        if k == 0:
+            for d in (2, -2, 1, -1):
+                send(b1, d, at(0, 0), part.b, place.along_z(d))
+        elif k < 7:
+            b1[-b_slots[k]].wait_recv()
+            if k in (3, 4):
+                side, d = SIDES[k - 3]
+                send(b1, 4 * d, at(0, -2 * d), part.b_half[side], place.along_z(2 * d))
+                send(b1, 3 * d, at(0, -2 * d), part.b, place.along_z(d))
+        else:
+            b1[4].wait_recv()
+            b1[-4].wait_recv()
+
+    def b2_step(h, k):
+        for side, d in SIDES:
             if h == 2:
                 b2[1, k, d].wait_recv()
             piece = part.b_half[side] if h == 2 else part.b
-            send(b2, (h, k, d), at(-d * (h - 1), b_order[k]), piece, place.along_y(d))
-
-    def a1_step(i):
-        if i == 0:
-            for d in (1, -1):
-                send(a1, (1, d), at(0, 0), part.a, place.along_y(d))
-        elif i in (1, 2):
-            side, d = i - 1, (1, -1)[i - 1]
-            a1[1, d].wait_recv()
-            send(a1, (2, d), at(-d, 0), part.a_half[side], place.along_y(d))
-        elif i == 3:
-            for d in (1, -1):
-                a1[2, d].wait_recv()
-
-    def b1_step(i):
-        if i == 0:
-            for d in (1, -1):
-                send(b1, (1, d), at(0, 0), part.b, place.along_z(d))
-        elif i in range(1, 7):
-            h, side = (i + 1) // 2, (i + 1) % 2
-            d = (1, -1)[side]
-            b1[h, d].wait_recv()
-            piece = part.b_half[side] if h == 3 else part.b
-            send(b1, (h + 1, d), at(0, -d * h), piece, place.along_z(d))
-        elif i == 7:
-            for d in (1, -1):
-                b1[4, d].wait_recv()
+            send(b2, (h, k, d), at(-d * (h - 1), b_slots[k]), piece, place.along_y(d))
 
     def step(i):
-        b1_step(i)
-        a1_step(i)
-        b2_step(i)
-        a2_step(i)
+        for order, width, first, second in (
+            (b_order, part.b[1], b1_step, b2_step),
+            (A_ORDER, part.a[1], a1_step, a2_step),
+        ):
+            if width:
+                h, k = order[i]
+                if h == 1:
+                    first(k)
+                second(h, k)
 
     def last():
-        for k in range(4):
-            for d in (1, -1):
-                a2[4, k, d].wait_recv()
-        for k in range(8):
-            for d in (1, -1):
-                b2[2, k, d].wait_recv()
+        for book, h, slots in ((a2, 4, a_slots), (b2, 2, b_slots)):
+            if book:
+                for k in range(len(slots)):
+                    for _, d in SIDES:
+                        book[h, k, d].wait_recv()
 
     return [functools.partial(step, i) for i in range(16)] + [last]
 
 
 def scatter_steps(place, start, part_sums, result, land_a, land_b, part):
     a1, b1, a2, b2 = {}, {}, {}, {}
-    a_order = (2, 1, -1, 0)
-    b_order = (4, 3, -3, 2, -2, 1, -1, 0)
+    a_slots = (2, 1, -1, 0)
+    b_slots = (4, 3, -3, 2, -2, 1, -1, 0)
+    b_order = [(1, k) for k in range(4)]
+    b_order += [(2, 0), (1, 4), (2, 1), (1, 5), (2, 2), (1, 6), (2, 3), (1, 7)] + [(2, k) for k in range(4, 8)]
     at = place.slot
-    used = {"a": 0, "b": 0}
+    used = {"a": {}, "b": {}}
 
     def send(book, key, slot, piece, to, kind):
         land = land_a if kind == "a" else land_b
-        index, offset = used[kind], piece[0] - (part.a if kind == "a" else part.b)[0]
-        used[kind] += 1
-        target = land.at[index, :, pl.ds(offset, piece[1])]
-        book[key] = (start(cols(part_sums, slot, piece), target, to), target, piece)
+        offset = piece[0] - (part.a if kind == "a" else part.b)[0]
+        index = used[kind].setdefault(key, len(used[kind]))
+
+        def there():
+            return land.at[index, :, pl.ds(offset, piece[1])]
+
+        book[key] = (start(lambda: cols(part_sums, slot, piece), there, to), there, piece)
 
     def add(book, key, slot):
-        copy, target, piece = book[key]
+        copy, there, piece = book[key]
         copy.wait_recv()
         own = cols(part_sums, slot, piece)
-        own[...] += target[...]
-
-    def a1_step(i):
-        h, k = i // 4 + 1, i % 4
-        for side, d in enumerate((1, -1)):
-            slot = at(a_order[k], d * (5 - h))
+        own[...] += there()[...]
+
+    def a1_step(h, k, sides=SIDES):
+        for side, d in sides:
+            slot = at(a_slots[k], d * (5 - h))
             if h > 1:
                 add(a1, (h - 1, k, d), slot)
             piece = part.a_half[side] if h == 1 else part.a
             send(a1, (h, k, d), slot, piece, place.along_z(d), "a")
 
-    def b1_step(i):
-        h, k = i // 8 + 1, i % 8
-        for side, d in enumerate((1, -1)):
-            slot = at(d * (3 - h), b_order[k])
+    def b1_step(h, k, sides=SIDES):
+        for side, d in sides:
+            slot = at(d * (3 - h), b_slots[k])
             if h == 2:
                 add(b1, (1, k, d), slot)
             piece = part.b_half[side] if h == 1 else part.b
             send(b1, (h, k, d), slot, piece, place.along_y(d), "b")
 
     def a1_end(k):
-        for d in (1, -1):
-            add(a1, (4, k, d), at(a_order[k], 0))
+        for _, d in SIDES:
+            add(a1, (4, k, d), at(a_slots[k], 0))
 
     def b1_end(k):
-        for d in (1, -1):
-            add(b1, (2, k, d), at(0, b_order[k]))
-
-    def a2_step(h):
-        for side, d in enumerate((1, -1)):
-            slot = at(d * (3 - h), 0)
-            if h == 2:
-                add(a2, (1, d), slot)
-            send(a2, (h, d), slot, part.a_half[side] if h == 1 else part.a, place.along_y(d), "a")
-
-    def b2_step(h):
-        for side, d in enumerate((1, -1)):
-            slot = at(0, d * (5 - h))
-            if h > 1:
-                add(b2, (h - 1, d), slot)
-            send(b2, (h, d), slot, part.b_half[side] if h == 1 else part.b, place.along_z(d), "b")
-
-    def end(book, key, piece):
+        for _, d in SIDES:
+            add(b1, (2, k, d), at(0, b_slots[k]))
+
+    def a2_step(k):
+        d = a_slots[k]
+        send(a2, d, at(d, 0), part.a, place.along_y(d), "a")
+
+    def b2_step(k):
+        d = b_slots[k]
+        if d == 4:
+            for side, way in SIDES:
+                send(b2, 4 * way, at(0, 4), part.b_half[side], place.along_z(2 * way), "b")
+            return
+        if abs(d) == 2:
+            add(b2, 2 * d, at(0, d))
+            add(b2, 3 * d // 2, at(0, d))
+        send(b2, d, at(0, d), part.b, place.along_z(d // 3 if abs(d) == 3 else d), "b")
+
+    def end(book, keys, piece):
         own = at(0, 0)
-        for d in (1, -1):
-            add(book, key + (d,), own)
+        for key in keys:
+            add(book, key, own)
         cols(result, own, piece)[...] = cols(part_sums, own, piece)[...]
+
+    early = SIDES[:1]
+
+    def before():
+        for k in range(4):
+            if part.a[1]:
+                a1_step(1, k, early)
+            else:
+                b1_step(1, k, early)
 
     def step(i):
         if i < 16:
-            a1_step(i)
-        if 0 <= i - SHIFT < 16:
-            b1_step(i - SHIFT)
-        if 0 <= i - SHIFT - 10 < 8:
-            b1_end(i - SHIFT - 10)
-        if 0 <= i - 14 < 4:
-            a1_end(i - 14)
-        if i - SHIFT in (10, 12, 14, 16):
-            b2_step((i - SHIFT - 8) // 2)
-        if i in (14, 16):
-            a2_step((i - 12) // 2)
-        if i == 18:
-            end(a2, (2,), part.a)
-        if i - SHIFT == 18:
-            end(b2, (4,), part.b)
-
-    return [functools.partial(step, i) for i in range(19 + SHIFT)]
-
-
-GATHER_WIRES = 4 + 8 + 32 + 32
-SCATTER_WIRES = 32 + 32 + 4 + 8
+            late = SIDES[1:] if i < 4 else SIDES
+            if part.b[1]:
+                b1_step(*b_order[i], SIDES if part.a[1] else late)
+            if part.a[1]:
+                a1_step(*A_ORDER[i], late)
+        for k in range(8):
+            if part.b[1] and i == b_order.index((2, k)) + 2:
+                b1_end(k)
+                if k < 7:
+                    b2_step(k)
+        for k in range(4):
+            if part.a[1] and i == A_ORDER.index((4, k)) + 2:
+                a1_end(k)
+                if k < 3:
+                    a2_step(k)
+        if i == 19:
+            if part.b[1]:
+                end(b2, (2, -2, 1, -1), part.b)
+            if part.a[1]:
+                end(a2, (2, 1, -1), part.a)
+
+    return [before], [functools.partial(step, i) for i in range(20)]
+
+
+GATHER_WIRES = 3 + 8 + 32 + 32
+SCATTER_WIRES = 32 + 32 + 3 + 8
 OTHER_WIRES = 11 + 24 + 4
 WIRES = GATHER_WIRES + SCATTER_WIRES + OTHER_WIRES
 
@@ -296,7 +337,7 @@
 def block_pieces(body, begin, end, size):
     def piece(first, last):
         def run():
-            @pl.loop(first, last)
+            @pl.loop(first, last, unroll=last - first)
             def _(c):
                 body(column_block(c))
 
@@ -322,8 +363,27 @@
     send, recv, local,
 ):
     place = Place()
-    wires = Wires(send, recv)
-    start = wires.range(GATHER_WIRES + SCATTER_WIRES, OTHER_WIRES)
+    wires = Wires(send, recv, POOL, OTHER_POOL)
+    core_wires = [Wires(send, recv, 0, POOL) for _ in PARTS]
+    other_start = wires.range(GATHER_WIRES + SCATTER_WIRES, OTHER_WIRES)
+
+    def start(src, dst, to):
+        return other_start(lambda: src, lambda: dst, to)
+
+    def by_core(lists):
+        def both(steps):
+            def run():
+                for index, step in enumerate(steps):
+                    pl.when(core_index == index)(step)
+
+            return run
+
+        return [both(steps) for steps in zip(*lists, strict=True)]
+
+    def gather(buf):
+        return by_core(
+            [gather_steps(place, w.range(0, GATHER_WIRES), buf, part) for w, part in zip(core_wires, PARTS)]
+        )
     f, t, y, z, x, core_index = place.f, place.t, place.y, place.z, place.x, place.c
 
     loads = [
@@ -361,7 +421,7 @@
 
     blocks = N // BLOCK
     loads[0].wait()
-    timed = at_times(gather_steps(place, wires.range(0, GATHER_WIRES), q_all, PART), 0)
+    timed = at_times(gather(q_all), 0)
     timed += [(1.4, loaded)]
     timed += at_times(block_pieces(split_block, 0, blocks, 1), 1.5)
     in_order(timed)
@@ -408,9 +468,16 @@
     def coefficients(at):
         w_part[:, :, at] = dot3(pt_split, (b_high[:, at], b_low[:, at])).reshape(F, R, BLOCK)
 
-    a_blocks = -(-PART.a[1] // BLOCK)
-    for piece in block_pieces(coefficients, 0, a_blocks, a_blocks):
-        piece()
+    scatters = [
+        scatter_steps(place, w.range(GATHER_WIRES, SCATTER_WIRES), w_part, w_all, land_a, land_b, part)
+        for w, part in zip(core_wires, PARTS)
+    ]
+    before, after = (by_core(lists) for lists in zip(*scatters))
+    (early,) = block_pieces(coefficients, 0, EARLY, EARLY)
+    (late,) = block_pieces(coefficients, EARLY, blocks, blocks)
+    early()
+    before[0]()
+    late()
 
     def summed(ref, count):
         total = ref[0]
@@ -455,7 +522,8 @@
 
     def gram_5():
         arrived()
-        wires.drain(gram_sent)
+        for copy in gram_sent:
+            copy.wait_send()
         row = lax.broadcasted_iota(jnp.int32, (RANK, RANK), 0)
         lane = lax.broadcasted_iota(jnp.int32, (RANK, RANK), 1)
         work[:, :, RANK:] = jnp.where(row == lane, 1.0, 0.0).astype(f32).reshape(F, R, RANK)
@@ -511,14 +579,10 @@
         squares = part * part
         norm_sum[...] += squares[:, :128] + squares[:, 128:]
 
-    lanes = wires.range(GATHER_WIRES, SCATTER_WIRES)
-    steps = scatter_steps(place, lanes, w_part, w_all, land_a, land_b, PART)
-    steps += gather_steps(place, wires.range(0, GATHER_WIRES), w_all, PART)
-    timed = at_times(steps, 0)
-    timed += at_times(block_pieces(coefficients, a_blocks, blocks, blocks), SHIFT - 0.9)
-    timed += [(4.5, gram_1), (7.5, gram_2), (11.5, gram_3), (14.5, gram_4), (16.5, gram_5)]
-    timed += at_times([panels(p, p + 2) for p in range(0, RANK // NB, 2)], 17.5)
-    timed += [(26.5, orthogonal)]
+    timed = at_times(after + gather(w_all), 0)
+    timed += [(5.5, gram_1), (8.5, gram_2), (12.5, gram_3), (15.5, gram_4), (17.5, gram_5)]
+    timed += at_times([panels(p, p + 1) for p in range(RANK // NB)], 18.5)
+    timed += [(35.5, orthogonal)]
     in_order(timed)
 
     stores = []
@@ -546,6 +610,7 @@
     for copy in stores:
         copy.wait()
     wires.drain()
+    by_core([[w.drain] for w in core_wires])[0]()
 
 
 def core_call(momentum, gradient, basis):
@@ -565,8 +630,8 @@
             pltpu.VMEM((F, R, N), f32),
             pltpu.VMEM((F, R, N), f32),
             pltpu.VMEM((F, R, N), f32),
-            pltpu.VMEM((A_LANDS, R, PART.a[1]), f32),
-            pltpu.VMEM((B_LANDS, R, PART.b[1]), f32),
+            pltpu.VMEM((A_LANDS, R, max(part.a[1] for part in PARTS)), f32),
+            pltpu.VMEM((B_LANDS, R, max(part.b[1] for part in PARTS)), f32),
             pltpu.VMEM((M, N), f32),
             pltpu.VMEM((M, N), bf16),
             pltpu.VMEM((M, N), bf16),
@@ -587,7 +652,7 @@
             pltpu.VMEM((RANK, 128), f32),
             pltpu.VMEM((2, 16, 128), f32),
             pltpu.VMEM((4, 16, 128), f32),
-            pltpu.SemaphoreType.DMA((POOL,)),
+            pltpu.SemaphoreType.DMA((POOL + OTHER_POOL,)),
             pltpu.SemaphoreType.DMA((WIRES,)),
             pltpu.SemaphoreType.DMA((3,)),
         ],
@@ -598,7 +663,8 @@
     )(momentum, gradient, basis)
 
 
-def update(momentum, gradient, coeffs, ortho, inverse, new_momentum, step):
+def update(momentum, gradient, coeffs, ortho, inverse, own_basis, new_momentum, step, new_basis):
+    new_basis[...] = own_basis[...]
     buffer = momentum[...] + gradient[...].astype(f32)
     high, low = split(coeffs[...])
     basis = ortho[...]
@@ -608,7 +674,7 @@
     step[...] = dot3(scaled, (high, low)).astype(bf16)
 
 
-def update_call(momentum, gradient, coeffs, ortho, inverse):
+def update_call(momentum, gradient, coeffs, ortho, inverse, own_basis):
     wide = N // 2
 
     def block(rows):
@@ -617,21 +683,26 @@
     return pl.pallas_call(
         update,
         grid=(N // wide,),
-        out_shape=(jax.ShapeDtypeStruct((M, N), f32), jax.ShapeDtypeStruct((M, N), bf16)),
+        out_shape=(
+            jax.ShapeDtypeStruct((M, N), f32),
+            jax.ShapeDtypeStruct((M, N), bf16),
+            jax.ShapeDtypeStruct((R, N), f32),
+        ),
         in_specs=[
             block(M), block(M), block(RANK),
             pl.BlockSpec((M, RANK), lambda c: (0, 0)),
             pl.BlockSpec((8, RANK), lambda c: (0, 0)),
+            block(R),
         ],
-        out_specs=(block(M), block(M)),
+        out_specs=(block(M), block(M), block(R)),
         compiler_params=pltpu.CompilerParams(vmem_limit_bytes=60 * 2**20),
         name="update",
-    )(momentum, gradient, coeffs, ortho, inverse)
+    )(momentum, gradient, coeffs, ortho, inverse, own_basis)
 
 
 def on_device(momentum, gradient, basis):
-    coeffs, ortho, inverse, new_basis = core_call(momentum, gradient, basis)
-    new_momentum, step = update_call(momentum, gradient, coeffs, ortho, inverse)
+    coeffs, ortho, inverse, own_basis = core_call(momentum, gradient, basis)
+    new_momentum, step, new_basis = update_call(momentum, gradient, coeffs, ortho, inverse, own_basis)
     return (new_momentum, new_basis, step)
 
 

time: 126 us -> 118 us (0.937)
  Pallas kernels: 125 us -> 117 us
    pallas_call x1, Pallas kernels: 119 us -> 111 us  [core_call(): pl.pallas_call(core, out_shape=(jax.ShapeDtypeStruct((RANK, N), f32), jax...]
where the time goes in v3:
time: 118 us
  Pallas kernels  117 us (99%)
    pallas_call x1, Pallas kernels, core_call(): pl.pallas_call(core, out_shape=(jax.ShapeDtypeStruct((RANK, N), f32), jax...  111 us
    pallas_call x1, Pallas kernels, update_call(): pl.pallas_call(update, grid=(N // wide,), out_shape=(jax.ShapeDtypeStruct...  5.87 us

profile of v3, /device:TPU:1, one launch (start us, length us, event | category | flops | bytes accessed | tf_op | source)
XLA Modules:
  0.0 117.6 jit_solution(16416682080857563743)
XLA Ops:
  0.6 111.1 %core.1 = (f32[256,3328]{1,0:T(8,128)}, f32[256,256]{1,0:T(8,128)}, f32[8,256]{1,0:T(8,128)}, f32[8,3328]{1,0:T(8,128)}) custom-call(f32[256,3328]{1,0:T(8,128)} %momentum.3, bf16[256,3328]{1,0:T(8,128)(2,1)} %gradient.3, f32[8,3328]{1,0:T(8,128)} %basis.1), custom_call_target="tpu_custom_call" | custom-call | tf_op jit(solution)/shard_map/core/pallas_call | solution.py:619
  111.7 5.9 %update.1 = (f32[256,3328]{1,0:T(8,128)}, bf16[256,3328]{1,0:T(8,128)(2,1)}, f32[8,3328]{1,0:T(8,128)}) custom-call(f32[256,3328]{1,0:T(8,128)} %momentum.3, bf16[256,3328]{1,0:T(8,128)(2,1)} %gradient.3, f32[256,3328]{1,0:T(8,128)} %get-tuple-element.10.coeffs, f32[256,256]{1,0:T(8,128)} %get-tuple-element.11.ortho, f32[8,256]{1,0:T(8,128)} %get-tuple-element.12.inverse, ...), custom_call_target="tpu_custom_call" | custom-call | tf_op jit(solution)/shard_map/update/pallas_call | solution.py:683

commit v4 on v3

--- a/solution.py
+++ b/solution.py
@@ -568,8 +568,7 @@
 
         return run
 
-    def orthogonal():
-        ortho[...] = exact(p_all[...].reshape(M, RANK), linv[...].reshape(RANK, RANK), ((1,), (1,)))
+    def prepare():
         linv_high[...], linv_low[...] = split(linv[...].reshape(RANK, RANK))
         norm_sum[...] = jnp.zeros_like(norm_sum)
 
@@ -582,7 +581,7 @@
     timed = at_times(after + gather(w_all), 0)
     timed += [(5.5, gram_1), (8.5, gram_2), (12.5, gram_3), (15.5, gram_4), (17.5, gram_5)]
     timed += at_times([panels(p, p + 1) for p in range(RANK // NB)], 18.5)
-    timed += [(35.5, orthogonal)]
+    timed += [(35.5, prepare)]
     in_order(timed)
 
     stores = []
@@ -598,6 +597,7 @@
     copy.wait_recv()
     norm_x[x] = norm_core[0] + norm_core[1]
     copies = [start(norm_x.at[x], norm_x.at[x], place.along_x(d)) for d in (2, 1, 3)]
+    ortho[...] = exact(p_all[...].reshape(M, RANK), linv[...].reshape(RANK, RANK), ((1,), (1,)))
     for copy in copies:
         copy.wait_recv()
     scale = lax.rsqrt((norm_x[0] + norm_x[1]) + (norm_x[2] + norm_x[3]) + norm_eps)

time: 118 us -> 118 us (level)
  no operation moved by 1% of the time
where the time goes in v4:
time: 118 us; the launch traced here: 117 us
  Pallas kernels  117 us (99%)
    pallas_call x1, Pallas kernels, core_call(): pl.pallas_call(core, out_shape=(jax.ShapeDtypeStruct((RANK, N), f32), jax...  111 us
    pallas_call x1, Pallas kernels, update_call(): pl.pallas_call(update, grid=(N // wide,), out_shape=(jax.ShapeDtypeStruct...  5.89 us

profile of v4, /device:TPU:1, one launch (start us, length us, event | category | flops | bytes accessed | tf_op | source)
XLA Modules:
  0.0 117.4 jit_solution(1230003335553460632)
XLA Ops:
  0.6 110.9 %core.1 = (f32[256,3328]{1,0:T(8,128)}, f32[256,256]{1,0:T(8,128)}, f32[8,256]{1,0:T(8,128)}, f32[8,3328]{1,0:T(8,128)}) custom-call(f32[256,3328]{1,0:T(8,128)} %momentum.3, bf16[256,3328]{1,0:T(8,128)(2,1)} %gradient.3, f32[8,3328]{1,0:T(8,128)} %basis.1), custom_call_target="tpu_custom_call" | custom-call | tf_op jit(solution)/shard_map/core/pallas_call | solution.py:619
  111.5 5.9 %update.1 = (f32[256,3328]{1,0:T(8,128)}, bf16[256,3328]{1,0:T(8,128)(2,1)}, f32[8,3328]{1,0:T(8,128)}) custom-call(f32[256,3328]{1,0:T(8,128)} %momentum.3, bf16[256,3328]{1,0:T(8,128)(2,1)} %gradient.3, f32[256,3328]{1,0:T(8,128)} %get-tuple-element.10.coeffs, f32[256,256]{1,0:T(8,128)} %get-tuple-element.11.ortho, f32[8,256]{1,0:T(8,128)} %get-tuple-element.12.inverse, ...), custom_call_target="tpu_custom_call" | custom-call | tf_op jit(solution)/shard_map/update/pallas_call | solution.py:683

commit v5 on v4

--- a/solution.py
+++ b/solution.py
@@ -35,7 +35,7 @@
         return (part[0], first), (part[0] + first, part[1] - first)
 
 
-PARTS = (Part(0, N, 2432), Part(0, N, 0))
+PARTS = (Part(0, N, 2560), Part(0, N, 0))
 A_LANDS = 4 * 4 * 2 + 2 * 2
 B_LANDS = 2 * 8 * 2 + 4 * 2
 POOL = 32
@@ -453,6 +453,20 @@
 
     proj = p_all[...].reshape(M, RANK)
     p_t[...] = proj.T
+    pt_split = split(p_t[...])
+
+    def coefficients(at):
+        w_part[:, :, at] = dot3(pt_split, (b_high[:, at], b_low[:, at])).reshape(F, R, BLOCK)
+
+    scatters = [
+        scatter_steps(place, w.range(GATHER_WIRES, SCATTER_WIRES), w_part, w_all, land_a, land_b, part)
+        for w, part in zip(core_wires, PARTS)
+    ]
+    before, after = (by_core(lists) for lists in zip(*scatters))
+    (early,) = block_pieces(coefficients, 0, EARLY, EARLY)
+    (late,) = block_pieces(coefficients, EARLY, blocks, blocks)
+    early()
+    before[0]()
     rows = p_t[pl.ds(pl.multiple_of(t * (RANK // T), RANK // T), RANK // T), :]
     own = exact(rows, proj)
     for j in range(Z):
@@ -462,21 +476,6 @@
     ]
     gram_sent = list(gram_copies)
     gram_z[z] = gram_own[z]
-
-    pt_split = split(p_t[...])
-
-    def coefficients(at):
-        w_part[:, :, at] = dot3(pt_split, (b_high[:, at], b_low[:, at])).reshape(F, R, BLOCK)
-
-    scatters = [
-        scatter_steps(place, w.range(GATHER_WIRES, SCATTER_WIRES), w_part, w_all, land_a, land_b, part)
-        for w, part in zip(core_wires, PARTS)
-    ]
-    before, after = (by_core(lists) for lists in zip(*scatters))
-    (early,) = block_pieces(coefficients, 0, EARLY, EARLY)
-    (late,) = block_pieces(coefficients, EARLY, blocks, blocks)
-    early()
-    before[0]()
     late()
 
     def summed(ref, count):
@@ -579,8 +578,8 @@
         norm_sum[...] += squares[:, :128] + squares[:, 128:]
 
     timed = at_times(after + gather(w_all), 0)
-    timed += [(5.5, gram_1), (8.5, gram_2), (12.5, gram_3), (15.5, gram_4), (17.5, gram_5)]
-    timed += at_times([panels(p, p + 1) for p in range(RANK // NB)], 18.5)
+    timed += [(7.5, gram_1), (10.5, gram_2), (14.5, gram_3), (17.5, gram_4), (19.5, gram_5)]
+    timed += at_times([panels(p, p + 1) for p in range(RANK // NB)], 20.5, 0.95)
     timed += [(35.5, prepare)]
     in_order(timed)
 

time: 118 us -> 118 us (level)
  no operation moved by 1% of the time
where the time goes in v5:
time: 118 us
  Pallas kernels  117 us (99%)
    pallas_call x1, Pallas kernels, core_call(): pl.pallas_call(core, out_shape=(jax.ShapeDtypeStruct((RANK, N), f32), jax...  111 us
    pallas_call x1, Pallas kernels, update_call(): pl.pallas_call(update, grid=(N // wide,), out_shape=(jax.ShapeDtypeStruct...  5.88 us

profile of v5, /device:TPU:1, one launch (start us, length us, event | category | flops | bytes accessed | tf_op | source)
XLA Modules:
  0.0 117.7 jit_solution(15889473243127502837)
XLA Ops:
  0.6 111.1 %core.1 = (f32[256,3328]{1,0:T(8,128)}, f32[256,256]{1,0:T(8,128)}, f32[8,256]{1,0:T(8,128)}, f32[8,3328]{1,0:T(8,128)}) custom-call(f32[256,3328]{1,0:T(8,128)} %momentum.3, bf16[256,3328]{1,0:T(8,128)(2,1)} %gradient.3, f32[8,3328]{1,0:T(8,128)} %basis.1), custom_call_target="tpu_custom_call" | custom-call | tf_op jit(solution)/shard_map/core/pallas_call | solution.py:618
  111.8 5.9 %update.1 = (f32[256,3328]{1,0:T(8,128)}, bf16[256,3328]{1,0:T(8,128)(2,1)}, f32[8,3328]{1,0:T(8,128)}) custom-call(f32[256,3328]{1,0:T(8,128)} %momentum.3, bf16[256,3328]{1,0:T(8,128)(2,1)} %gradient.3, f32[256,3328]{1,0:T(8,128)} %get-tuple-element.10.coeffs, f32[256,256]{1,0:T(8,128)} %get-tuple-element.11.ortho, f32[8,256]{1,0:T(8,128)} %get-tuple-element.12.inverse, ...), custom_call_target="tpu_custom_call" | custom-call | tf_op jit(solution)/shard_map/update/pallas_call | solution.py:682
